TPU v7x, 128 devices: a whole 4x4x4 slice. The times are simulated.
128 devices in a mesh: row: 8 (over y, z_hi), col: 16 (over z_lo, x, core).
Axes of the slice: x: 4, y: 4, z: 4 (z_hi: 2, z_lo: 2; z = z_hi * 2 + z_lo), core: 2. Of those that a mesh axis runs over, the one named last changes fastest.
Arguments:
- base: bfloat16 [2, 8192, 29568], P(None, ('row', 'col')), may hold values from -21 to 21
- adjusted: bfloat16 [2, 8192, 29568], P(None, ('row', 'col')), may hold values from -21 to 21
- omega: bfloat16 [29568, 512], P('col'), may hold values from -0.03125 to 0.03125
Outputs:
- basis: float32 [2, 8192, 512], P(None, ('row', 'col'))
- projected: float32 [2, 512, 29568], P(None, 'row', 'col')
All inputs are finite; a program needn't handle non-finite values.
Results may differ from a plain program's by a relative error of at most 0.005.
Values may be sent and summed in bfloat16 or wider, within the bound.
A program may use at most 128 MiB of HBM per device.

v0:
```python
import math

import jax
import jax.numpy as jnp
from jax import lax
from jax.sharding import PartitionSpec as P

D = 8192


def factor_basis(gram, sketch_rows):
    lower = jnp.linalg.cholesky(gram)
    return lax.linalg.triangular_solve(
        lower, sketch_rows, left_side=False, lower=True, transpose_a=True
    )


def body(base, adjusted, omega):
    grid_base, grid_adjusted = (
        lax.all_to_all(base, "col", split_axis=2, concat_axis=1, tiled=True),
        lax.all_to_all(adjusted, "col", split_axis=2, concat_axis=1, tiled=True),
    )
    delta = (grid_adjusted.astype(jnp.float32) - grid_base.astype(jnp.float32)).astype(jnp.bfloat16)
    rows_part = delta
    sketch_own = lax.psum_scatter(
        jnp.einsum("mkf,fr->kmr", rows_part, omega, preferred_element_type=jnp.float32),
        "col",
        scatter_dimension=0,
        tiled=True,
    )
    local_gram = jnp.einsum("kmr,kms->mrs", sketch_own, sketch_own, precision=lax.Precision.HIGHEST)
    gram = lax.psum(local_gram, ("row", "col")) / D
    basis = factor_basis(gram, jnp.transpose(sketch_own, (1, 0, 2)))
    basis_low = basis.astype(jnp.bfloat16)
    rows_part = delta
    partial_proj = jnp.einsum(
        "osg,osn->ogn",
        lax.all_gather(basis_low, "col", axis=1, tiled=True),
        rows_part,
        preferred_element_type=jnp.float32,
    )
    projected = lax.psum_scatter(partial_proj, "row", scatter_dimension=1, tiled=True) / math.sqrt(
        D
    )
    return (basis, projected)


def solution(mesh):
    placed = (P(None, ("row", "col"), None), P(None, ("row", "col"), None), P("col", None))
    return jax.shard_map(
        body,
        mesh=mesh,
        in_specs=placed,
        out_specs=(P(None, ("row", "col"), None), P(None, "row", "col")),
        check_vma=False,
    )
```

profile of v0, /device:TPU:1, one launch (start us, length us, event | category | flops | bytes accessed | tf_op | source)
XLA Modules:
  0.0 1015.7 jit_solution(15558125382904513296)
XLA Ops:
  7.2 31.1 %copy.54 = bf16[2,64,29568]{1,0,2:T(2,128)(2,1)} copy(bf16[2,64,29568]{2,1,0:T(8,128)(2,1)} %param.3) | data formatting | bytes 15138816 | tf_op args[0]
  38.3 17.4 %reshape.84 = bf16[16,2,118272]{2,1,0:T(2,128)(2,1)} reshape(bf16[29568,2,64]{2,1,0:T(2,128)(2,1)} %bitcast.79) | data formatting | bytes 15138816
  55.6 7.2 all-to-all-start.1
  62.8 30.9 %copy.53 = bf16[2,64,29568]{1,0,2:T(2,128)(2,1)} copy(bf16[2,64,29568]{2,1,0:T(8,128)(2,1)} %param.4) | data formatting | bytes 15138816 | tf_op args[1]
  93.8 17.4 %reshape.86 = bf16[16,2,118272]{2,1,0:T(2,128)(2,1)} reshape(bf16[29568,2,64]{2,1,0:T(2,128)(2,1)} %bitcast.80) | data formatting | bytes 15138816
  111.2 53.2 %all-to-all-done.1 = bf16[16,2,118272]{2,1,0:T(2,128)(2,1)} async-done(((bf16[16,2,118272]{2,1,0:T(2,128)(2,1)}), bf16[16,2,118272]{2,1,0:T(2,128)(2,1)}, u32[]{:S(2)}, u32[]{:S(2)}) %all-to-all-start.1) | async-done | bytes 7569440 | tf_op jit(solution)/shard_map/all_to_all | solution.py:20
  164.4 5.0 all-to-all-start
  169.4 17.2 %reshape.85 = bf16[29568,2,64]{2,1,0:T(2,128)(2,1)} reshape(bf16[16,2,118272]{2,1,0:T(2,128)(2,1)} %all-to-all-done.1) | data formatting | bytes 15138816
  186.7 84.0 %all-to-all-done = bf16[16,2,118272]{2,1,0:T(2,128)(2,1)} async-done(((bf16[16,2,118272]{2,1,0:T(2,128)(2,1)}), bf16[16,2,118272]{2,1,0:T(2,128)(2,1)}, u32[]{:S(2)}, u32[]{:S(2)}) %all-to-all-start) | async-done | bytes 7569440 | tf_op jit(solution)/shard_map/all_to_all | solution.py:21
  270.7 17.3 %reshape.87 = bf16[29568,2,64]{2,1,0:T(2,128)(2,1)} reshape(bf16[16,2,118272]{2,1,0:T(2,128)(2,1)} %all-to-all-done) | data formatting | bytes 15138816
  288.0 18.8 %subtract_convert_fusion = bf16[2,64,29568]{1,0,2:T(2,128)(2,1)} fusion(bf16[29568,2,64]{2,1,0:T(2,128)(2,1)} %reshape.87, bf16[29568,2,64]{2,1,0:T(2,128)(2,1)} %reshape.85), kind=kLoop, calls=%fused_computation.2 | loop fusion | flops 15138816 | bytes 22708224 | tf_op jit(solution)/shard_map/convert
  306.8 31.2 %copy.55 = bf16[2,64,16,1848]{3,1,2,0:T(8,128)(2,1)} copy(bf16[2,64,16,1848]{1,0,3,2:T(2,128)(2,1)} %bitcast.78) | data formatting | bytes 15138816 | tf_op jit(solution)/shard_map/sub | solution.py:23
  338.0 9.3 convolution_bitcast_fusion
  347.4 64.4 %reduce-scatter.3.cloned.1.call-done = f32[64,2,512]{2,0,1:T(8,128)} async-done(((f32[1024,2,512]{2,0,1:T(8,128)}), f32[64,2,512]{2,0,1:T(8,128)}) %reduce-scatter.3.cloned.1.call-update) | async-done | bytes 262160 | tf_op jit(solution)/shard_map/reduce_scatter | solution.py:25
  411.8 4.2 fusion.33
  416.2 153.4 %all-reduce.3.cloned.1.call-done = f32[2,512,512]{1,2,0:T(8,128)} async-done(((f32[2,512,512]{1,2,0:T(8,128)}), f32[2,512,512]{1,2,0:T(8,128)}) %all-reduce.3.cloned.1.call-update) | async-done | bytes 2097168 | tf_op jit(solution)/shard_map/psum | solution.py:32
  569.6 3.2 broadcast_multiply_fusion
  572.8 3.4 copy.58
  580.3 23.5 %custom-call.34 = f32[2,128,128]{2,1,0:T(8,128)S(1)} custom-call(f32[2,128,128]{2,1,0:T(8,128)S(1)} %cholesky.274), custom_call_target="Cholesky" | custom-call | tf_op jit(solution)/shard_map/jit(cholesky)/cholesky | solution.py:12
  603.8 19.7 %custom-call.35 = f32[2,1,128,128]{2,3,1,0:T(8,128)S(1)} custom-call(f32[2,1,128,128]{3,2,1,0:T(8,128)S(1)} %select_bitcast_fusion.2), custom_call_target="InvertDiagBlocksLowerTriangular" | custom-call | tf_op jit(solution)/shard_map/jit(cholesky)/cholesky | solution.py:12
  628.9 23.5 %custom-call.36 = f32[2,128,128]{2,1,0:T(8,128)S(1)} custom-call(f32[2,128,128]{2,1,0:T(8,128)S(1)} %cholesky.278), custom_call_target="Cholesky" | custom-call | tf_op jit(solution)/shard_map/jit(cholesky)/cholesky | solution.py:12
  653.0 19.8 %custom-call.37 = f32[2,1,128,128]{2,3,1,0:T(8,128)S(1)} custom-call(f32[2,1,128,128]{3,2,1,0:T(8,128)S(1)} %get-tuple-element.29), custom_call_target="InvertDiagBlocksLowerTriangular" | custom-call | tf_op jit(solution)/shard_map/jit(cholesky)/cholesky | solution.py:12
  675.8 23.5 %custom-call.38 = f32[2,128,128]{2,1,0:T(8,128)S(1)} custom-call(f32[2,128,128]{2,1,0:T(8,128)S(1)} %cholesky.283), custom_call_target="Cholesky" | custom-call | tf_op jit(solution)/shard_map/jit(cholesky)/cholesky | solution.py:12
  699.9 19.7 %custom-call.39 = f32[2,1,128,128]{2,3,1,0:T(8,128)S(1)} custom-call(f32[2,1,128,128]{3,2,1,0:T(8,128)S(1)} %get-tuple-element.27), custom_call_target="InvertDiagBlocksLowerTriangular" | custom-call | tf_op jit(solution)/shard_map/jit(cholesky)/cholesky | solution.py:12
  722.3 23.7 %custom-call.40 = f32[2,128,128]{2,1,0:T(8,128)S(1)} custom-call(f32[2,128,128]{2,1,0:T(8,128)S(1)} %convolution_subtract_fusion.2), custom_call_target="Cholesky" | custom-call | tf_op jit(solution)/shard_map/jit(cholesky)/cholesky | solution.py:12
  747.0 3.5 select_select_fusion
  750.5 13.7 %while.1 = (s32[]{:T(128)}, f32[2,512,512]{2,1,0:T(8,128)}, s32[4,2]{0,1:T(2,128)S(1)}, f32[4,2,128,128]{3,2,0,1:T(8,128)}, s32[]{:T(128)}) while((s32[]{:T(128)}, f32[2,512,512]{2,1,0:T(8,128)}, s32[4,2]{0,1:T(2,128)S(1)}, f32[4,2,128,128]{3,2,0,1:T(8,128)}, s32[]{:T(128)}) %tuple.33), condition=%wide.while_cond, body=%wide.while_body.sunk | while | flops 2 | bytes 263777 | solution.py:13
  751.1 2.9 bitcast_dynamic-update-slice_fusion.2
  764.2 79.4 %custom-call.41 = f32[2,4,128,128]{2,3,1,0:T(8,128)S(1)} custom-call(f32[2,4,128,128]{3,2,1,0:T(8,128)} %bitcast.87), custom_call_target="InvertDiagBlocksLowerTriangular" | custom-call | tf_op jit(solution)/shard_map/triangular_solve | solution.py:13
  850.0 32.6 %all-gather.2.cloned.1.call-done = bf16[2,1024,512]{2,1,0:T(8,128)(2,1)} async-done(((bf16[2,64,512]{2,1,0:T(8,128)(2,1)}), bf16[2,1024,512]{2,1,0:T(8,128)(2,1)}) %all-gather.2.cloned.1.call-update) | async-done | bytes 2097168 | tf_op jit(solution)/shard_map/all_gather | solution.py:38
  882.6 11.6 %fusion.34 = f32[2,512,1848]{2,1,0:T(8,128)} fusion(bf16[2,1024,512]{2,1,0:T(8,128)(2,1)} %all-gather.2.cloned.1.call-done, bf16[2,1024,1848]{2,1,0:T(8,128)(2,1)} %bitcast.82), kind=kOutput, calls=%fused_computation.75 | convolution fusion | flops 3875536896 | bytes 17235968 | tf_op jit(solution)/shard_map/osg,osn->ogn/dot_general | solution.py:36
  894.2 112.5 %reduce-scatter.5.cloned.1.call-done = f32[2,64,1848]{2,1,0:T(8,128)} async-done(((f32[2,512,1848]{2,1,0:T(8,128)}), f32[2,64,1848]{2,1,0:T(8,128)}) %reduce-scatter.5.cloned.1.call-update) | async-done | bytes 946192 | tf_op jit(solution)/shard_map/reduce_scatter | solution.py:42
  (58 shorter events, 37.3 us)
Async XLA Ops:
  7.2 330.8 %copy-start = (bf16[1848,512]{1,0:T(8,128)(2,1)S(1)}, bf16[1848,512]{1,0:T(8,128)(2,1)}, u32[]{:S(2)}) copy-start(bf16[1848,512]{1,0:T(8,128)(2,1)} %param.5) | copy-start | bytes 5677060
  55.6 108.7 %all-to-all-start.1 = ((bf16[16,2,118272]{2,1,0:T(2,128)(2,1)}), bf16[16,2,118272]{2,1,0:T(2,128)(2,1)}, u32[]{:S(2)}, u32[]{:S(2)}) async-start(bf16[16,2,118272]{2,1,0:T(2,128)(2,1)} %reshape.84), calls=%async_computation.1 | async-start | bytes 15138816 | tf_op jit(solution)/shard_map/all_to_all | solution.py:20
  164.4 106.4 %all-to-all-start = ((bf16[16,2,118272]{2,1,0:T(2,128)(2,1)}), bf16[16,2,118272]{2,1,0:T(2,128)(2,1)}, u32[]{:S(2)}, u32[]{:S(2)}) async-start(bf16[16,2,118272]{2,1,0:T(2,128)(2,1)} %reshape.86), calls=%async_computation | async-start | bytes 15138816 | tf_op jit(solution)/shard_map/all_to_all | solution.py:21
  169.4 242.4 %reduce-scatter.3.cloned.1.call-start = ((), (), s32[]{:S(2)}) async-start(), calls=%async_computation.4 | async-start | bytes 4456448 | tf_op jit(solution)/shard_map/reduce_scatter | solution.py:25
  347.3 222.2 %all-reduce.3.cloned.1.call-start = ((), (), s32[]{:S(2)}) async-start(), calls=%async_computation.5 | async-start | bytes 4194304 | tf_op jit(solution)/shard_map/psum | solution.py:32
  416.0 466.6 %all-gather.2.cloned.1.call-start = ((), (), s32[]{:S(2)}) async-start(), calls=%async_computation.6 | async-start | bytes 2228224 | tf_op jit(solution)/shard_map/all_gather | solution.py:38
  578.9 1.4 copy-start.1
  747.0 96.6 %copy-start.2 = (f32[64,2,512]{2,0,1:T(8,128)S(1)}, f32[64,2,512]{2,0,1:T(8,128)}, u32[]{:S(2)}) copy-start(f32[64,2,512]{2,0,1:T(8,128)} %reduce-scatter.3.cloned.1.call-done) | copy-start | bytes 786436
  849.7 156.9 %reduce-scatter.5.cloned.1.call-start = ((), (), s32[]{:S(2)}) async-start(), calls=%async_computation.7 | async-start | bytes 8847360 | tf_op jit(solution)/shard_map/reduce_scatter | solution.py:42
Sparse Core Ops, SparseCore 0:
  347.5 64.2 reduce-scatter.2
  416.6 152.9 all-reduce.2
  849.9 32.6 all-gather.1
  894.3 112.3 reduce-scatter.4
where the time goes:
time: 1030 us; the launch traced here: 1020 us
  waiting for transfers between devices  500 us (49%)
  other arithmetic  266 us (26%)
  local copies, waits for them, and re-layouts  183 us (18%)
  matrix products  39.7 us (4%)
  between operations  14.2 us (1%)
  starting transfers between devices  12.6 us (1%)
    another operation x16, other arithmetic, factor_basis(): lower = jnp.linalg.cholesky(gram)  156 us
    psum x1, waiting for transfers between devices, body(): gram = lax.psum(local_gram, ('row', 'col')) / D  153 us
    unnamed x12, local copies, waits for them, and re-layouts  133 us
    reduce_scatter x1, waiting for transfers between devices, body(): lax.psum_scatter(partial_proj, 'row', scatter_dimension=1, tiled=True)  112 us
    all_to_all x1, waiting for transfers between devices, body(): lax.all_to_all(adjusted, 'col', split_axis=2, concat_axis=1, tiled=True)  84 us
    another operation x4, other arithmetic, factor_basis(): lax.linalg.triangular_solve(lower, sketch_rows, left_side=False, lower=Tr...  83 us
    reduce_scatter x1, waiting for transfers between devices, body(): lax.psum_scatter(jnp.einsum('mkf,fr->kmr', rows_part, omega, preferred_el...  64.4 us
    all_to_all x1, waiting for transfers between devices, body(): lax.all_to_all(base, 'col', split_axis=2, concat_axis=1, tiled=True)  53.2 us
  transfers between devices with their start and end apart: 6, of which 6 were waited for; matrix products, arithmetic and copies ran while one was open for 6% of the time, Pallas kernels for 0%

commit v1 on v0

v1 whole, which is shorter than its diff:
```python
import math

import jax
import jax.numpy as jnp
from jax import lax
from jax.experimental import pallas as pl
from jax.experimental.pallas import tpu as pltpu
from jax.sharding import PartitionSpec as P

MESH = pl.DeviceIdType.MESH
HIGH = lax.Precision.HIGHEST
D = 8192
FF = 29568
R = 512
MATS = 2
ROWS = 64
BLOCK = 1848
WIDE = 1920
WINDOW = 2048
STAGES = 4
COLS = 16
TILE = 128
HEIGHTS = (32, 24, 16, 8)
STARTS = (0, 32, 56, 72)
SLAB = 80


def f32(x):
    return x.astype(jnp.float32)


def dot_nt(a, b, precision=None):
    return lax.dot_general(
        a, b, (((1,), (1,)), ((), ())), precision=precision, preferred_element_type=jnp.float32
    )


def dot_tn(a, b, precision=None):
    return lax.dot_general(
        a, b, (((0,), (0,)), ((), ())), precision=precision, preferred_element_type=jnp.float32
    )


def dot_nn(a, b, precision=None):
    return jnp.dot(a, b, precision=precision, preferred_element_type=jnp.float32)


def invert_factor(block):
    count = TILE // 8
    rows = [block[8 * i : 8 * i + 8, :] for i in range(count)]
    shape = (8, TILE)
    lane = lax.broadcasted_iota(jnp.int32, shape, 1)
    sub = lax.broadcasted_iota(jnp.int32, shape, 0)
    for s in range(count):
        cols = {
            (i, j): jnp.broadcast_to(rows[i][:, 8 * s + j : 8 * s + j + 1], shape)
            for i in range(s, count)
            for j in range(8)
        }
        for j in range(8):
            here = lane == 8 * s + j
            pivot = jnp.broadcast_to(cols[s, j][j : j + 1, :], shape)
            inverse = 1.0 / pivot
            row = jnp.where(here, 1.0, jnp.broadcast_to(rows[s][j : j + 1, :], shape))
            heads = {
                j2: jnp.broadcast_to(cols[s, j2][j : j + 1, :], shape) for j2 in range(j + 1, 8)
            }
            for i in range(s, count):
                factor = cols[i, j] * inverse
                clear = here
                if i == s:
                    factor = jnp.where(sub > j, factor, 0.0)
                    clear = here & (sub > j)
                rows[i] = jnp.where(clear, 0.0, rows[i]) - factor * row
                for j2 in range(j + 1, 8):
                    cols[i, j2] = cols[i, j2] - factor * heads[j2]
    out = []
    for i in range(count):
        at = sub + 8 * i
        diagonal = jnp.sum(jnp.where(lane == at, rows[i], 0.0), axis=1, keepdims=True)
        unit = jnp.where(lane < at, rows[i], jnp.where(lane == at, 1.0, 0.0))
        out.append(unit * (1.0 / jnp.sqrt(diagonal)))
    return jnp.concatenate(out, axis=0)


def kernel(
    base_ref, adjusted_ref, omega_ref, basis_ref, projected_ref,
    old, new, source, held, omega_pad, keep, odd, pre, part, rows_all,
    gram, packed, slabs, total, across, spread, low, inv, basis_t, out_part, in_part,
    load_sem, send_sem, recv_sem, odd_send, odd_recv, part_send, part_recv,
    rows_send, rows_recv, core_send, core_recv, slab_send, slab_recv, x_send, x_recv,
    spread_send, spread_recv, inv_send, inv_recv, out_send, out_recv,
):
    r, c = lax.axis_index("row"), lax.axis_index("col")
    y, z_hi = r // 2, r % 2
    z_lo, x, k = c // 8, (c // 2) % 4, c % 2
    z = z_hi * 2 + z_lo
    q = y * 4 + z

    def col_of(z_lo_, x_, k_):
        return z_lo_ * 8 + x_ * 2 + k_

    def partner_col(i, sign):
        dx, dz, dk = i // 4, (i // 2) % 2, i % 2
        return col_of((z_lo + dz) % 2, (x + sign * dx + 4) % 4, (k + dk) % 2)

    def plane(q_):
        y_, z_ = q_ // 4, q_ % 4
        return (y_ * 2 + z_ // 2, col_of(z_ % 2, x, k))

    def xor(a, d, bits):
        out = 0
        for bit in range(bits):
            own = (a // (1 << bit)) % 2
            out = out + ((own + (d // (1 << bit)) % 2) % 2) * (1 << bit)
        return out

    twin = (r, col_of(z_lo, x, 1 - k))

    def window(f):
        first = (BLOCK * f) // TILE
        start = jnp.minimum(first, (FF - WINDOW) // TILE)
        return start, first - start, BLOCK * f - first * TILE

    def loads(i):
        start, _, _ = window(partner_col(i, 1))
        span = pl.ds(pl.multiple_of(start * TILE, TILE), WINDOW)
        slot = i % STAGES
        return [
            pltpu.make_async_copy(
                src.at[:, :, span], dst.at[slot, :, :, pl.ds(0, WINDOW)], load_sem.at[n, slot]
            )
            for n, (src, dst) in enumerate(((base_ref, old), (adjusted_ref, new)))
        ]

    for i in range(STAGES):
        for copy in loads(i):
            copy.start()

    barrier = pltpu.get_barrier_semaphore()
    for i in range(1, COLS):
        pl.semaphore_signal(
            barrier, inc=1, device_id=(r, partner_col(i, 1)), device_id_type=MESH
        )
    for d in range(1, COLS):
        pl.semaphore_signal(barrier, inc=1, device_id=plane(xor(q, d, 4)), device_id_type=MESH)

    omega_pad[0:1840, :] = omega_ref[0:1840, :]
    tail = f32(omega_ref[1840:1848, :])
    omega_pad[1840:1856, :] = jnp.concatenate([tail, jnp.zeros_like(tail)], axis=0).astype(
        jnp.bfloat16
    )
    omega_pad[1856:1920, :] = jnp.zeros((64, R), jnp.bfloat16)

    lane = lax.broadcasted_iota(jnp.int32, (ROWS, TILE), 1)

    def shifted(i, put):
        _, skip, ahead = window(partner_col(i, 1))
        slot = i % STAGES
        turn = (TILE - ahead) % TILE
        for m in range(MATS):
            last = None
            for t in range(16):
                span = pl.ds(pl.multiple_of((t + skip) * TILE, TILE), TILE)
                tile = f32(new[slot, m, :, span]) - f32(old[slot, m, :, span])
                tile = pltpu.roll(tile, turn, 1)
                if t > 0:
                    value = jnp.where(lane < TILE - ahead, last, tile)
                    if t == 15:
                        value = jnp.where(lane < BLOCK - 14 * TILE, value, 0.0)
                    put(m, (t - 1) * TILE, value.astype(jnp.bfloat16))
                last = tile

    def put_own(m, at, value):
        held[m, 0, :, at : at + TILE] = value

    for copy in loads(0):
        copy.wait()
    shifted(0, put_own)
    for copy in loads(STAGES):
        copy.start()
    pl.semaphore_wait(barrier, 2 * (COLS - 1))

    def delta_copy(m, i):
        return pltpu.make_async_remote_copy(
            src_ref=source.at[m, i],
            dst_ref=held.at[m, i],
            send_sem=send_sem.at[m, i],
            recv_sem=recv_sem.at[m, i],
            device_id=(r, partner_col(i, 1)),
            device_id_type=MESH,
        )

    def send_step(i, carry):
        for copy in loads(i):
            copy.wait()

        def put(m, at, value):
            source[m, i, :, at : at + TILE] = value

        shifted(i, put)

        @pl.when(i + STAGES < COLS)
        def _():
            for copy in loads(i + STAGES):
                copy.start()

        for m in range(MATS):
            delta_copy(m, i).start()
        return carry

    lax.fori_loop(1, COLS, send_step, 0)

    def odd_copy(m, g):
        return pltpu.make_async_remote_copy(
            src_ref=odd.at[m, g],
            dst_ref=pre.at[m, g],
            send_sem=odd_send.at[m, g],
            recv_sem=odd_recv.at[m, g],
            device_id=twin,
            device_id_type=MESH,
        )

    def part_copy(m, e):
        dx, dz = e // 2, e % 2
        to = (r, col_of((z_lo + dz) % 2, (x - dx + 4) % 4, k))
        return pltpu.make_async_remote_copy(
            src_ref=keep.at[m, e],
            dst_ref=part.at[m, e],
            send_sem=part_send.at[m, e],
            recv_sem=part_recv.at[m, e],
            device_id=to,
            device_id_type=MESH,
        )

    def sketch(m, g):
        block = held[m, pl.ds(4 * g, 4)].reshape(4 * ROWS, WIDE)
        got = dot_nn(block, omega_pad[...]).reshape(4, ROWS, R)
        keep[m, 2 * g] = got[0]
        odd[m, g, 0] = got[1]
        keep[m, 2 * g + 1] = got[2]
        odd[m, g, 1] = got[3]
        odd_copy(m, g).start()

    def hand_on(m, g):
        odd_copy(m, g).wait_recv()
        for h in range(2):
            keep[m, 2 * g + h] = keep[m, 2 * g + h] + pre[m, g, h]

    for m in range(MATS):
        for i in range(1, 4):
            delta_copy(m, i).wait_recv()
        sketch(m, 0)

    def sketch_step(g, carry):
        for m in range(MATS):
            for i in range(4):
                delta_copy(m, 4 * g + i).wait_recv()
            sketch(m, g)
        for m in range(MATS):
            hand_on(m, g - 1)
            for h in range(2):
                @pl.when(2 * (g - 1) + h > 0)
                def _():
                    part_copy(m, 2 * (g - 1) + h).start()
        return carry

    lax.fori_loop(1, 4, sketch_step, 0)
    for m in range(MATS):
        hand_on(m, 3)
        for h in range(2):
            part_copy(m, 6 + h).start()

    for m in range(MATS):
        value = keep[m, 0]
        for e in range(1, 8):
            part_copy(m, e).wait_recv()
            value = value + part[m, e]
        rows_all[0, m] = value

    def rows_core(e):
        return pltpu.make_async_remote_copy(
            src_ref=rows_all.at[2 * e],
            dst_ref=rows_all.at[2 * e + 1],
            send_sem=core_send.at[e],
            recv_sem=core_recv.at[e],
            device_id=twin,
            device_id_type=MESH,
        )

    def rows_copy(e):
        dx, dz = e // 2, e % 2
        to = (r, col_of((z_lo + dz) % 2, (x + dx) % 4, k))
        return pltpu.make_async_remote_copy(
            src_ref=rows_all.at[0],
            dst_ref=rows_all.at[2 * e],
            send_sem=rows_send.at[e],
            recv_sem=rows_recv.at[e],
            device_id=to,
            device_id_type=MESH,
        )

    rows_core(0).start()
    for e in range(1, 8):
        rows_copy(e).start()

    rows_core(0).wait_recv()
    mine = jnp.concatenate([rows_all[0, k], rows_all[1, k]], axis=0)
    gram[...] = dot_tn(mine, mine, HIGH) * (1.0 / D)
    for p in range(16):
        for j in range(4):
            h, at = HEIGHTS[j], STARTS[j]
            top = TILE * j + p * h
            packed[p, at : at + h, :] = gram[top : top + h, TILE * j : TILE * j + TILE]

    def slab_copy(d):
        to = xor(q, d, 4)
        return pltpu.make_async_remote_copy(
            src_ref=packed.at[to],
            dst_ref=slabs.at[d],
            send_sem=slab_send.at[d],
            recv_sem=slab_recv.at[d],
            device_id=plane(to),
            device_id_type=MESH,
        )

    for d in range(1, 16):
        slab_copy(d).start()
    value = packed[q]
    for d in range(1, 16):
        slab_copy(d).wait_recv()
        value = value + slabs[d]
    total[...] = value

    def x_copy(d):
        return pltpu.make_async_remote_copy(
            src_ref=total,
            dst_ref=across.at[d],
            send_sem=x_send.at[d],
            recv_sem=x_recv.at[d],
            device_id=(r, col_of(z_lo, xor(x, d, 2), k)),
            device_id_type=MESH,
        )

    for d in range(1, 4):
        x_copy(d).start()
    for d in range(1, 4):
        x_copy(d).wait_recv()
    spread[q] = (total[...] + across[1]) + (across[2] + across[3])

    def spread_copy(d):
        return pltpu.make_async_remote_copy(
            src_ref=spread.at[q],
            dst_ref=spread.at[q],
            send_sem=spread_send.at[d],
            recv_sem=spread_recv.at[d],
            device_id=plane(xor(q, d, 4)),
            device_id_type=MESH,
        )

    def spread_arrival(d):
        other = xor(q, d, 4)
        return pltpu.make_async_remote_copy(
            src_ref=spread.at[other],
            dst_ref=spread.at[other],
            send_sem=spread_send.at[d],
            recv_sem=spread_recv.at[d],
            device_id=plane(other),
            device_id_type=MESH,
        )

    for d in range(1, 16):
        spread_copy(d).start()
    for e in range(1, 8):
        rows_copy(e).wait_recv()
        rows_core(e).start()
    for d in range(1, 16):
        spread_arrival(d).wait_recv()

    gram[...] = jnp.zeros((R, R), jnp.float32)
    for p in range(16):
        for j in range(4):
            h, at = HEIGHTS[j], STARTS[j]
            top = TILE * j + p * h
            gram[top : top + h, TILE * j : TILE * j + TILE] = spread[p, at : at + h, :]

    low[...] = jnp.zeros((R, R), jnp.float32)
    inv[k] = jnp.zeros((R, R), jnp.float32)
    row_at = lax.broadcasted_iota(jnp.int32, (R, TILE), 0)

    def factor_step(b, carry):
        span = pl.ds(pl.multiple_of(b * TILE, TILE), TILE)
        own = invert_factor(gram[span, span])
        panel = dot_nt(gram[:, span], own, HIGH)
        panel = jnp.where(row_at >= (b + 1) * TILE, panel, 0.0)
        done = dot_nn(low[span, :], inv[k], HIGH)
        inv[k, span, :] = -dot_nn(own, done, HIGH)
        inv[k, span, span] = own
        low[:, span] = panel
        gram[...] = gram[...] - dot_nt(panel, panel, HIGH)
        return carry

    lax.fori_loop(0, R // TILE, factor_step, 0)

    inv_copy = pltpu.make_async_remote_copy(
        src_ref=inv.at[k],
        dst_ref=inv.at[k],
        send_sem=inv_send,
        recv_sem=inv_recv,
        device_id=twin,
        device_id_type=MESH,
    )
    inv_arrival = pltpu.make_async_remote_copy(
        src_ref=inv.at[1 - k],
        dst_ref=inv.at[1 - k],
        send_sem=inv_send,
        recv_sem=inv_recv,
        device_id=twin,
        device_id_type=MESH,
    )
    inv_copy.start()
    for e in range(1, 8):
        rows_core(e).wait_recv()
    inv_arrival.wait_recv()

    def out_copy(m, d):
        to = xor(r, d, 3)
        return pltpu.make_async_remote_copy(
            src_ref=out_part.at[m, to],
            dst_ref=in_part.at[m, d],
            send_sem=out_send.at[m, d],
            recv_sem=out_recv.at[m, d],
            device_id=(to, c),
            device_id_type=MESH,
        )

    for m in range(MATS):
        basis_t[...] = dot_nt(inv[m], rows_all[:, m].reshape(COLS * ROWS, R), HIGH).astype(
            jnp.bfloat16
        )

        def project_step(n, carry):
            span = pl.ds(pl.multiple_of(n * 384, TILE), 384)
            block = held[m, :, :, span].reshape(COLS * ROWS, 384)
            got = dot_nn(basis_t[...], block)
            out_part[m, :, :, span] = got.reshape(8, ROWS, 384).astype(jnp.bfloat16)
            return carry

        lax.fori_loop(0, WIDE // 384, project_step, 0)
        for d in range(1, 8):
            out_copy(m, d).start()

    for m in range(MATS):
        basis_ref[m] = dot_nt(rows_all[0, m], inv[m], HIGH)

    for m in range(MATS):
        for d in range(1, 8):
            out_copy(m, d).wait_recv()
        value = f32(out_part[m, r])
        for d in range(1, 8):
            value = value + f32(in_part[m, d])
        projected_ref[m] = value[:, :BLOCK] * (1.0 / math.sqrt(D))

    for m in range(MATS):
        for i in range(1, COLS):
            delta_copy(m, i).wait_send()
        for g in range(4):
            odd_copy(m, g).wait_send()
        for e in range(1, 8):
            part_copy(m, e).wait_send()
        for d in range(1, 8):
            out_copy(m, d).wait_send()
    for e in range(8):
        rows_core(e).wait_send()
    for e in range(1, 8):
        rows_copy(e).wait_send()
    for d in range(1, 16):
        slab_copy(d).wait_send()
        spread_copy(d).wait_send()
    for d in range(1, 4):
        x_copy(d).wait_send()
    inv_copy.wait_send()


def body(base, adjusted, omega):
    f, b16, sem = jnp.float32, jnp.bfloat16, pltpu.SemaphoreType.DMA
    any_space, vmem = pl.BlockSpec(memory_space=pl.ANY), pl.BlockSpec(memory_space=pltpu.VMEM)
    scratch = [
        pltpu.VMEM((STAGES, MATS, ROWS, WINDOW + TILE), b16),
        pltpu.VMEM((STAGES, MATS, ROWS, WINDOW + TILE), b16),
        pltpu.VMEM((MATS, COLS, ROWS, WIDE), b16),
        pltpu.VMEM((MATS, COLS, ROWS, WIDE), b16),
        pltpu.VMEM((WIDE, R), b16),
        pltpu.VMEM((MATS, 8, ROWS, R), f),
        pltpu.VMEM((MATS, 4, 2, ROWS, R), f),
        pltpu.VMEM((MATS, 4, 2, ROWS, R), f),
        pltpu.VMEM((MATS, 8, ROWS, R), f),
        pltpu.VMEM((COLS, MATS, ROWS, R), f),
        pltpu.VMEM((R, R), f),
        pltpu.VMEM((16, SLAB, TILE), f),
        pltpu.VMEM((16, SLAB, TILE), f),
        pltpu.VMEM((SLAB, TILE), f),
        pltpu.VMEM((4, SLAB, TILE), f),
        pltpu.VMEM((16, SLAB, TILE), f),
        pltpu.VMEM((R, R), f),
        pltpu.VMEM((MATS, R, R), f),
        pltpu.VMEM((R, COLS * ROWS), b16),
        pltpu.VMEM((MATS, 8, ROWS, WIDE), b16),
        pltpu.VMEM((MATS, 8, ROWS, WIDE), b16),
        sem((2, STAGES)),
        sem((MATS, COLS)), sem((MATS, COLS)),
        sem((MATS, 4)), sem((MATS, 4)),
        sem((MATS, 8)), sem((MATS, 8)),
        sem((8,)), sem((8,)),
        sem((8,)), sem((8,)),
        sem((16,)), sem((16,)),
        sem((4,)), sem((4,)),
        sem((16,)), sem((16,)),
        sem, sem,
        sem((MATS, 8)), sem((MATS, 8)),
    ]
    return pl.pallas_call(
        kernel,
        out_shape=(
            jax.ShapeDtypeStruct((MATS, ROWS, R), f),
            jax.ShapeDtypeStruct((MATS, ROWS, BLOCK), f),
        ),
        in_specs=[any_space, any_space, vmem],
        out_specs=(vmem, vmem),
        scratch_shapes=scratch,
        compiler_params=pltpu.CompilerParams(
            collective_id=0, has_side_effects=True, vmem_limit_bytes=62 << 20
        ),
        cost_estimate=pl.CostEstimate(
            flops=10_000_000_000, bytes_accessed=20_000_000, transcendentals=0
        ),
        name="sketch_project",
    )(base, adjusted, omega)


def solution(mesh):
    placed = (P(None, ("row", "col"), None), P(None, ("row", "col"), None), P("col", None))
    return jax.shard_map(
        body,
        mesh=mesh,
        in_specs=placed,
        out_specs=(P(None, ("row", "col"), None), P(None, "row", "col")),
        check_vma=False,
    )
```

time: 1030 us -> 310 us (0.30); the launches traced: 1020 us -> 309 us
  waiting for transfers between devices: 500 us -> 0 us
  Pallas kernels: 0 us -> 305 us
  other arithmetic: 266 us -> 0 us
  local copies, waits for them, and re-layouts: 183 us -> 3.88 us
  matrix products: 39.7 us -> 0 us
  between operations: 14.2 us -> 0.64 us
  starting transfers between devices: 12.6 us -> 0 us
    pallas_call x0 -> x1, Pallas kernels: none -> 305 us  [body(): pl.pallas_call(kernel, out_shape=(jax.ShapeDtypeStruct((MATS, ROWS, R), f...]
    another operation x21 -> x0, other arithmetic: 257 us -> none  [the longest x16 156 us: factor_basis(): lower = jnp.linalg.cholesky(gram)]
    reduce_scatter x2 -> x0, waiting for transfers between devices: 177 us -> none  [the longest x1 112 us: body(): lax.psum_scatter(partial_proj, 'row', scatter_dimension=1, tiled=True)]
    psum x1 -> x0, waiting for transfers between devices: 153 us -> none  [body(): gram = lax.psum(local_gram, ('row', 'col')) / D]
    all_to_all x2 -> x0, waiting for transfers between devices: 137 us -> none  [the longest x1 84 us: body(): lax.all_to_all(adjusted, 'col', split_axis=2, concat_axis=1, tiled=True)]
    unnamed x12 -> x2, local copies, waits for them, and re-layouts: 133 us -> 3.88 us
    all_gather x1 -> x0, waiting for transfers between devices: 32.6 us -> none  [body(): lax.all_gather(basis_low, 'col', axis=1, tiled=True)]
    sub x1 -> x0, local copies, waits for them, and re-layouts: 31.2 us -> none  [body(): grid_adjusted.astype(jnp.float32) - grid_base.astype(jnp.float32)]
  transfers between devices with their start and end apart: 6 -> 0, of which waited for: 6 -> 0; matrix products, arithmetic and copies ran while one was open for 6% -> 0% of each run, Pallas kernels for 0% -> 0%
where the time goes in v1:
time: 310 us; the launch traced here: 309 us
  Pallas kernels  305 us (98%)
  local copies, waits for them, and re-layouts  3.88 us (1%)
    pallas_call x1, Pallas kernels, body(): pl.pallas_call(kernel, out_shape=(jax.ShapeDtypeStruct((MATS, ROWS, R), f...  305 us

profile of v1, /device:TPU:1, one launch (start us, length us, event | category | flops | bytes accessed | tf_op | source)
XLA Modules:
  0.0 309.3 jit_solution(500604199515808482)
XLA Ops:
  0.6 304.8 %sketch_project.1 = (f32[2,64,512]{2,1,0:T(8,128)}, f32[2,64,1848]{2,1,0:T(8,128)}) custom-call(bf16[2,64,29568]{2,1,0:T(8,128)(2,1)} %base_ref.1, bf16[2,64,29568]{2,1,0:T(8,128)(2,1)} %adjusted_ref.1, bf16[1848,512]{1,0:T(8,128)(2,1)} %omega_ref.1), custom_call_target="tpu_custom_call" | custom-call | flops 10000000000 | bytes 20000000 | tf_op jit(solution)/shard_map/sketch_project/pallas_call | solution.py:522
  305.4 1.7 copy.7
  307.1 2.2 copy.8

commit v2 on v1

--- a/solution.py
+++ b/solution.py
@@ -87,9 +87,9 @@
     base_ref, adjusted_ref, omega_ref, basis_ref, projected_ref,
     old, new, source, held, omega_pad, keep, odd, pre, part, rows_all,
     gram, packed, slabs, total, across, spread, low, inv, basis_t, out_part, in_part,
-    load_sem, send_sem, recv_sem, odd_send, odd_recv, part_send, part_recv,
+    load_sem, omega_send, omega_recv, own_sem, send_sem, recv_sem, odd_send, odd_recv, part_send, part_recv,
     rows_send, rows_recv, core_send, core_recv, slab_send, slab_recv, x_send, x_recv,
-    spread_send, spread_recv, inv_send, inv_recv, out_send, out_recv,
+    spread_send, spread_recv, inv_send, inv_recv, out_send, out_recv, own_out_sem,
 ):
     r, c = lax.axis_index("row"), lax.axis_index("col")
     y, z_hi = r // 2, r % 2
@@ -100,9 +100,35 @@
     def col_of(z_lo_, x_, k_):
         return z_lo_ * 8 + x_ * 2 + k_
 
-    def partner_col(i, sign):
-        dx, dz, dk = i // 4, (i // 2) % 2, i % 2
-        return col_of((z_lo + dz) % 2, (x + sign * dx + 4) % 4, (k + dk) % 2)
+    def offsets(s):
+        t, g, u, near = s % 3, s // 3, (s + 4) % 16, s // 12
+        dx = (1 + 2 * t - 3 * (t // 2)) * (1 - near)
+        dz = ((g + 1) % 2) * (1 - near) + ((u + 1) % 2) * near
+        dk = (g // 2) * (1 - near) + (((u + 1) // 2) % 2) * near
+        return dx, dz, dk
+
+    def place(m, s, sign):
+        dx, dz, dk = offsets(s)
+        y_ = (y + m * sign * dx + 4) % 4
+        x_ = (x + (1 - m) * sign * dx + 4) % 4
+        z_ = (z + dz * (2 * z_lo - 1) * (2 * m - 1) + 4) % 4
+        return x_, y_, z_, (k + dk) % 2
+
+    def device(x_, y_, z_, k_):
+        return (y_ * 2 + z_ // 2, col_of(z_ % 2, x_, k_))
+
+    def member(m, s, sign=1):
+        return device(*place(m, s, sign))
+
+    def turned(x_, y_, k_):
+        return (x_ + y_ * (1 - 2 * k_) + 4) % 4
+
+    def block_of(m, s):
+        x_, y_, z_, k_ = place(m, s, 1)
+        return col_of(z_ % 2, (1 - m) * x_ + m * turned(x_, y_, k_), k_)
+
+    mine_steps = (0, 1, 2, 3, 4, 5, 12, 15)
+    twin_steps = (6, 7, 8, 9, 10, 11, 14, 13)
 
     def plane(q_):
         y_, z_ = q_ // 4, q_ % 4
@@ -116,6 +142,15 @@
         return out
 
     twin = (r, col_of(z_lo, x, 1 - k))
+    pending = []
+
+    def finish():
+        for copy in pending:
+            copy.wait_send()
+
+        @pl.when(omega_sends > 0)
+        def _():
+            omega_copy(omega_to).wait_send()
 
     def window(f):
         first = (BLOCK * f) // TILE
@@ -123,42 +158,67 @@
         return start, first - start, BLOCK * f - first * TILE
 
     def loads(i):
-        start, _, _ = window(partner_col(i, 1))
-        span = pl.ds(pl.multiple_of(start * TILE, TILE), WINDOW)
-        slot = i % STAGES
-        return [
-            pltpu.make_async_copy(
-                src.at[:, :, span], dst.at[slot, :, :, pl.ds(0, WINDOW)], load_sem.at[n, slot]
-            )
-            for n, (src, dst) in enumerate(((base_ref, old), (adjusted_ref, new)))
-        ]
+        slot, out = i % STAGES, []
+        for m in range(MATS):
+            start, _, _ = window(block_of(m, i))
+            span = pl.ds(pl.multiple_of(start * TILE, TILE), WINDOW)
+            for n, (src, dst) in enumerate(((base_ref, old), (adjusted_ref, new))):
+                out.append(
+                    pltpu.make_async_copy(
+                        src.at[m, :, span],
+                        dst.at[slot, m, :, pl.ds(0, WINDOW)],
+                        load_sem.at[n, m, slot],
+                    )
+                )
+        return out
 
     for i in range(STAGES):
         for copy in loads(i):
             copy.start()
 
     barrier = pltpu.get_barrier_semaphore()
-    for i in range(1, COLS):
-        pl.semaphore_signal(
-            barrier, inc=1, device_id=(r, partner_col(i, 1)), device_id_type=MESH
-        )
+    def greet(to):
+        pl.semaphore_signal(barrier, inc=1, device_id=to, device_id_type=MESH)
+
+    for i in range(COLS - 1):
+        for m in range(MATS):
+            greet(member(m, i))
     for d in range(1, COLS):
-        pl.semaphore_signal(barrier, inc=1, device_id=plane(xor(q, d, 4)), device_id_type=MESH)
-
-    omega_pad[0:1840, :] = omega_ref[0:1840, :]
+        greet(plane(xor(q, d, 4)))
+
+    def owner(to):
+        return device(turned(x, y, k), to // 2, (to % 2) * 2 + z_lo, k)
+
+    def holder(of):
+        y_ = of // 2
+        return device((x - y_ * (1 - 2 * k) + 4) % 4, y_, (of % 2) * 2 + z_lo, k)
+
+    at_zero = 1 - (y + 3) // 4
+    for d in range(8):
+        to = xor(r, d, 3)
+        if d == 0:
+            @pl.when(y > 0)
+            def _():
+                greet(owner(to))
+                greet(holder(to))
+        else:
+            greet(owner(to))
+            greet(holder(to))
+
+    omega_pad[0, 0:1840, :] = omega_ref[0:1840, :]
     tail = f32(omega_ref[1840:1848, :])
-    omega_pad[1840:1856, :] = jnp.concatenate([tail, jnp.zeros_like(tail)], axis=0).astype(
+    omega_pad[0, 1840:1856, :] = jnp.concatenate([tail, jnp.zeros_like(tail)], axis=0).astype(
         jnp.bfloat16
     )
-    omega_pad[1856:1920, :] = jnp.zeros((64, R), jnp.bfloat16)
+    omega_pad[0, 1856:1920, :] = jnp.zeros((64, R), jnp.bfloat16)
 
     lane = lax.broadcasted_iota(jnp.int32, (ROWS, TILE), 1)
 
     def shifted(i, put):
-        _, skip, ahead = window(partner_col(i, 1))
         slot = i % STAGES
-        turn = (TILE - ahead) % TILE
         for m in range(MATS):
+            _, skip, ahead = window(block_of(m, i))
+            turn = (TILE - ahead) % TILE
             last = None
             for t in range(16):
                 span = pl.ds(pl.multiple_of((t + skip) * TILE, TILE), TILE)
@@ -171,15 +231,31 @@
                     put(m, (t - 1) * TILE, value.astype(jnp.bfloat16))
                 last = tile
 
-    def put_own(m, at, value):
-        held[m, 0, :, at : at + TILE] = value
-
-    for copy in loads(0):
-        copy.wait()
-    shifted(0, put_own)
-    for copy in loads(STAGES):
-        copy.start()
-    pl.semaphore_wait(barrier, 2 * (COLS - 1))
+    pl.semaphore_wait(barrier, 3 * (COLS - 1) + 16 - 2 * at_zero)
+
+    def omega_copy(to):
+        return pltpu.make_async_remote_copy(
+            src_ref=omega_pad.at[0],
+            dst_ref=omega_pad.at[1],
+            send_sem=omega_send,
+            recv_sem=omega_recv,
+            device_id=to,
+            device_id_type=MESH,
+        )
+
+    from_zero = (y // 2) * (1 - y % 2) * k
+    to_two = at_zero * k
+    omega_to = device((x - y * (1 - 2 * k) + 2 * to_two + 4) % 4, y + 2 * to_two, z, k)
+    omega_sends = (1 - at_zero) * (1 - from_zero) + to_two
+    own_omega = pltpu.make_async_copy(omega_pad.at[0], omega_pad.at[1], own_sem)
+
+    @pl.when(omega_sends > 0)
+    def _():
+        omega_copy(omega_to).start()
+
+    @pl.when(at_zero > 0)
+    def _():
+        own_omega.start()
 
     def delta_copy(m, i):
         return pltpu.make_async_remote_copy(
@@ -187,7 +263,7 @@
             dst_ref=held.at[m, i],
             send_sem=send_sem.at[m, i],
             recv_sem=recv_sem.at[m, i],
-            device_id=(r, partner_col(i, 1)),
+            device_id=member(m, i),
             device_id_type=MESH,
         )
 
@@ -209,12 +285,21 @@
             delta_copy(m, i).start()
         return carry
 
-    lax.fori_loop(1, COLS, send_step, 0)
+    lax.fori_loop(0, COLS - 1, send_step, 0)
+    pending += [delta_copy(m, i) for m in range(MATS) for i in range(COLS - 1)]
+
+    def put_own(m, at, value):
+        held[m, COLS - 1, :, at : at + TILE] = value
+
+    for copy in loads(COLS - 1):
+        copy.wait()
+    shifted(COLS - 1, put_own)
 
     def odd_copy(m, g):
-        return pltpu.make_async_remote_copy(
-            src_ref=odd.at[m, g],
-            dst_ref=pre.at[m, g],
+        span = pl.ds(6 * g, 6 - 4 * g)
+        return pltpu.make_async_remote_copy(
+            src_ref=odd.at[m, span],
+            dst_ref=pre.at[m, span],
             send_sem=odd_send.at[m, g],
             recv_sem=odd_recv.at[m, g],
             device_id=twin,
@@ -222,90 +307,98 @@
         )
 
     def part_copy(m, e):
-        dx, dz = e // 2, e % 2
-        to = (r, col_of((z_lo + dz) % 2, (x - dx + 4) % 4, k))
         return pltpu.make_async_remote_copy(
             src_ref=keep.at[m, e],
             dst_ref=part.at[m, e],
             send_sem=part_send.at[m, e],
             recv_sem=part_recv.at[m, e],
-            device_id=to,
-            device_id_type=MESH,
-        )
-
-    def sketch(m, g):
-        block = held[m, pl.ds(4 * g, 4)].reshape(4 * ROWS, WIDE)
-        got = dot_nn(block, omega_pad[...]).reshape(4, ROWS, R)
-        keep[m, 2 * g] = got[0]
-        odd[m, g, 0] = got[1]
-        keep[m, 2 * g + 1] = got[2]
-        odd[m, g, 1] = got[3]
-        odd_copy(m, g).start()
-
-    def hand_on(m, g):
-        odd_copy(m, g).wait_recv()
-        for h in range(2):
-            keep[m, 2 * g + h] = keep[m, 2 * g + h] + pre[m, g, h]
+            device_id=member(m, mine_steps[e], -1),
+            device_id_type=MESH,
+        )
+
+    def sketch(m, first, count):
+        for i in range(first, min(first + count, COLS - 1)):
+            delta_copy(m, i).wait_recv()
+        block = held[m, first : first + count].reshape(count * ROWS, WIDE)
+        return dot_nn(block, omega_pad[m]).reshape(count, ROWS, R)
+
+    def near_step(m, carry):
+        keep[m, 0:6] = sketch(m, 0, 6)
+        return carry
+
+    def far_step(m, carry):
+        odd[m, 0:6] = sketch(m, 6, 6)
+        odd_copy(m, 0).start()
+        return carry
+
+    def last_step(m, carry):
+        got = sketch(m, 12, 4)
+        odd[m, 6] = got[2]
+        odd[m, 7] = got[1]
+        odd_copy(m, 1).start()
+        keep[m, 6] = got[0]
+        keep[m, 7] = got[3]
+        odd_copy(m, 0).wait_recv()
+        for e in range(6):
+            keep[m, e] = keep[m, e] + pre[m, e]
+            part_copy(m, e).start()
+        return carry
+
+    def close_step(m, carry):
+        odd_copy(m, 1).wait_recv()
+        keep[m, 6] = keep[m, 6] + pre[m, 6]
+        part_copy(m, 6).start()
+        keep[m, 7] = keep[m, 7] + pre[m, 7]
+        return carry
+
+    near_step(0, 0)
+
+    @pl.when(at_zero > 0)
+    def _():
+        own_omega.wait()
+
+    @pl.when(at_zero == 0)
+    def _():
+        omega_copy(omega_to).wait_recv()
+
+    near_step(1, 0)
+    for step in (far_step, last_step, close_step):
+        lax.fori_loop(0, MATS, step, 0)
+    pending += [odd_copy(m, g) for m in range(MATS) for g in range(2)]
+    pending += [part_copy(m, e) for m in range(MATS) for e in range(7)]
 
     for m in range(MATS):
-        for i in range(1, 4):
-            delta_copy(m, i).wait_recv()
-        sketch(m, 0)
-
-    def sketch_step(g, carry):
-        for m in range(MATS):
-            for i in range(4):
-                delta_copy(m, 4 * g + i).wait_recv()
-            sketch(m, g)
-        for m in range(MATS):
-            hand_on(m, g - 1)
-            for h in range(2):
-                @pl.when(2 * (g - 1) + h > 0)
-                def _():
-                    part_copy(m, 2 * (g - 1) + h).start()
-        return carry
-
-    lax.fori_loop(1, 4, sketch_step, 0)
-    for m in range(MATS):
-        hand_on(m, 3)
-        for h in range(2):
-            part_copy(m, 6 + h).start()
-
-    for m in range(MATS):
-        value = keep[m, 0]
-        for e in range(1, 8):
+        value = keep[m, 7]
+        for e in range(7):
             part_copy(m, e).wait_recv()
             value = value + part[m, e]
-        rows_all[0, m] = value
+        rows_all[COLS - 1, m] = value
 
     def rows_core(e):
         return pltpu.make_async_remote_copy(
-            src_ref=rows_all.at[2 * e],
-            dst_ref=rows_all.at[2 * e + 1],
+            src_ref=rows_all.at[mine_steps[e]],
+            dst_ref=rows_all.at[twin_steps[e]],
             send_sem=core_send.at[e],
             recv_sem=core_recv.at[e],
             device_id=twin,
             device_id_type=MESH,
         )
 
-    def rows_copy(e):
-        dx, dz = e // 2, e % 2
-        to = (r, col_of((z_lo + dz) % 2, (x + dx) % 4, k))
-        return pltpu.make_async_remote_copy(
-            src_ref=rows_all.at[0],
-            dst_ref=rows_all.at[2 * e],
-            send_sem=rows_send.at[e],
-            recv_sem=rows_recv.at[e],
-            device_id=to,
-            device_id_type=MESH,
-        )
-
-    rows_core(0).start()
-    for e in range(1, 8):
-        rows_copy(e).start()
-
-    rows_core(0).wait_recv()
-    mine = jnp.concatenate([rows_all[0, k], rows_all[1, k]], axis=0)
+    def rows_copy(m, e):
+        return pltpu.make_async_remote_copy(
+            src_ref=rows_all.at[COLS - 1, m],
+            dst_ref=rows_all.at[mine_steps[e], m],
+            send_sem=rows_send.at[m, e],
+            recv_sem=rows_recv.at[m, e],
+            device_id=member(m, mine_steps[e]),
+            device_id_type=MESH,
+        )
+
+    rows_core(7).start()
+    pending.append(rows_core(7))
+
+    rows_core(7).wait_recv()
+    mine = jnp.concatenate([rows_all[15, k], rows_all[13, k]], axis=0)
     gram[...] = dot_tn(mine, mine, HIGH) * (1.0 / D)
     for p in range(16):
         for j in range(4):
@@ -326,6 +419,7 @@
 
     for d in range(1, 16):
         slab_copy(d).start()
+    pending += [slab_copy(d) for d in range(1, 16)]
     value = packed[q]
     for d in range(1, 16):
         slab_copy(d).wait_recv()
@@ -344,6 +438,7 @@
 
     for d in range(1, 4):
         x_copy(d).start()
+    pending += [x_copy(d) for d in range(1, 4)]
     for d in range(1, 4):
         x_copy(d).wait_recv()
     spread[q] = (total[...] + across[1]) + (across[2] + across[3])
@@ -371,11 +466,13 @@
 
     for d in range(1, 16):
         spread_copy(d).start()
-    for e in range(1, 8):
-        rows_copy(e).wait_recv()
-        rows_core(e).start()
+    pending += [spread_copy(d) for d in range(1, 16)]
     for d in range(1, 16):
         spread_arrival(d).wait_recv()
+    for e in range(7):
+        for m in range(MATS):
+            rows_copy(m, e).start()
+    pending += [rows_copy(m, e) for m in range(MATS) for e in range(7)]
 
     gram[...] = jnp.zeros((R, R), jnp.float32)
     for p in range(16):
@@ -398,9 +495,18 @@
         inv[k, span, span] = own
         low[:, span] = panel
         gram[...] = gram[...] - dot_nt(panel, panel, HIGH)
+
+        @pl.when(b == 2)
+        def _():
+            for e in range(7):
+                for m in range(MATS):
+                    rows_copy(m, e).wait_recv()
+                rows_core(e).start()
+
         return carry
 
     lax.fori_loop(0, R // TILE, factor_step, 0)
+    pending += [rows_core(e) for e in range(7)]
 
     inv_copy = pltpu.make_async_remote_copy(
         src_ref=inv.at[k],
@@ -419,7 +525,8 @@
         device_id_type=MESH,
     )
     inv_copy.start()
-    for e in range(1, 8):
+    pending.append(inv_copy)
+    for e in range(7):
         rows_core(e).wait_recv()
     inv_arrival.wait_recv()
 
@@ -427,17 +534,40 @@
         to = xor(r, d, 3)
         return pltpu.make_async_remote_copy(
             src_ref=out_part.at[m, to],
+            dst_ref=in_part.at[m, r],
+            send_sem=out_send.at[m, d],
+            recv_sem=out_recv.at[m, r],
+            device_id=owner(to) if m else (to, c),
+            device_id_type=MESH,
+        )
+
+    def out_arrival(m, d):
+        return pltpu.make_async_remote_copy(
+            src_ref=out_part.at[m, d],
             dst_ref=in_part.at[m, d],
-            send_sem=out_send.at[m, d],
+            send_sem=out_send.at[m, 0],
             recv_sem=out_recv.at[m, d],
-            device_id=(to, c),
-            device_id_type=MESH,
-        )
+            device_id=holder(d) if m else (d, c),
+            device_id_type=MESH,
+        )
+
+    own_out = [
+        pltpu.make_async_copy(out_part.at[m, r], in_part.at[m, r], own_out_sem.at[m])
+        for m in range(MATS)
+    ]
 
     for m in range(MATS):
-        basis_t[...] = dot_nt(inv[m], rows_all[:, m].reshape(COLS * ROWS, R), HIGH).astype(
-            jnp.bfloat16
-        )
+        factor, every = inv[m], rows_all[:, m].reshape(COLS * ROWS, R)
+        factor_hi, every_hi = factor.astype(jnp.bfloat16), every.astype(jnp.bfloat16)
+        factor_lo = (factor - f32(factor_hi)).astype(jnp.bfloat16)
+        every_lo = (every - f32(every_hi)).astype(jnp.bfloat16)
+        for i in range(R // TILE):
+            top, deep = TILE * i, TILE * (i + 1)
+            hi, lo = factor_hi[top:deep, :deep], factor_lo[top:deep, :deep]
+            basis_t[top:deep, :] = (
+                dot_nt(hi, every_hi[:, :deep])
+                + (dot_nt(hi, every_lo[:, :deep]) + dot_nt(lo, every_hi[:, :deep]))
+            ).astype(jnp.bfloat16)
 
         def project_step(n, carry):
             span = pl.ds(pl.multiple_of(n * 384, TILE), 384)
@@ -449,37 +579,45 @@
         lax.fori_loop(0, WIDE // 384, project_step, 0)
         for d in range(1, 8):
             out_copy(m, d).start()
+        if m:
+            @pl.when(at_zero > 0)
+            def _():
+                own_out[1].start()
+
+            @pl.when(at_zero == 0)
+            def _():
+                out_copy(1, 0).start()
+        else:
+            own_out[0].start()
+    pending += [out_copy(m, d) for m in range(MATS) for d in range(1, 8)]
 
     for m in range(MATS):
-        basis_ref[m] = dot_nt(rows_all[0, m], inv[m], HIGH)
+        basis_ref[m] = dot_nt(rows_all[COLS - 1, m], inv[m], HIGH)
 
     for m in range(MATS):
+        if m:
+            @pl.when(at_zero > 0)
+            def _():
+                own_out[1].wait()
+
+            @pl.when(at_zero == 0)
+            def _():
+                out_arrival(1, r).wait_recv()
+        else:
+            own_out[0].wait()
         for d in range(1, 8):
-            out_copy(m, d).wait_recv()
-        value = f32(out_part[m, r])
+            out_arrival(m, xor(r, d, 3)).wait_recv()
+        value = f32(in_part[m, 0])
         for d in range(1, 8):
             value = value + f32(in_part[m, d])
         projected_ref[m] = value[:, :BLOCK] * (1.0 / math.sqrt(D))
 
-    for m in range(MATS):
-        for i in range(1, COLS):
-            delta_copy(m, i).wait_send()
-        for g in range(4):
-            odd_copy(m, g).wait_send()
-        for e in range(1, 8):
-            part_copy(m, e).wait_send()
-        for d in range(1, 8):
-            out_copy(m, d).wait_send()
-    for e in range(8):
-        rows_core(e).wait_send()
-    for e in range(1, 8):
-        rows_copy(e).wait_send()
-    for d in range(1, 16):
-        slab_copy(d).wait_send()
-        spread_copy(d).wait_send()
-    for d in range(1, 4):
-        x_copy(d).wait_send()
-    inv_copy.wait_send()
+
+    @pl.when(at_zero == 0)
+    def _():
+        out_copy(1, 0).wait_send()
+
+    finish()
 
 
 def body(base, adjusted, omega):
@@ -490,10 +628,10 @@
         pltpu.VMEM((STAGES, MATS, ROWS, WINDOW + TILE), b16),
         pltpu.VMEM((MATS, COLS, ROWS, WIDE), b16),
         pltpu.VMEM((MATS, COLS, ROWS, WIDE), b16),
-        pltpu.VMEM((WIDE, R), b16),
+        pltpu.VMEM((MATS, WIDE, R), b16),
         pltpu.VMEM((MATS, 8, ROWS, R), f),
-        pltpu.VMEM((MATS, 4, 2, ROWS, R), f),
-        pltpu.VMEM((MATS, 4, 2, ROWS, R), f),
+        pltpu.VMEM((MATS, 8, ROWS, R), f),
+        pltpu.VMEM((MATS, 8, ROWS, R), f),
         pltpu.VMEM((MATS, 8, ROWS, R), f),
         pltpu.VMEM((COLS, MATS, ROWS, R), f),
         pltpu.VMEM((R, R), f),
@@ -507,17 +645,18 @@
         pltpu.VMEM((R, COLS * ROWS), b16),
         pltpu.VMEM((MATS, 8, ROWS, WIDE), b16),
         pltpu.VMEM((MATS, 8, ROWS, WIDE), b16),
-        sem((2, STAGES)),
+        sem((2, MATS, STAGES)),
+        sem, sem, sem,
         sem((MATS, COLS)), sem((MATS, COLS)),
-        sem((MATS, 4)), sem((MATS, 4)),
+        sem((MATS, 2)), sem((MATS, 2)),
         sem((MATS, 8)), sem((MATS, 8)),
-        sem((8,)), sem((8,)),
+        sem((MATS, 8)), sem((MATS, 8)),
         sem((8,)), sem((8,)),
         sem((16,)), sem((16,)),
         sem((4,)), sem((4,)),
         sem((16,)), sem((16,)),
         sem, sem,
-        sem((MATS, 8)), sem((MATS, 8)),
+        sem((MATS, 8)), sem((MATS, 8)), sem((MATS,)),
     ]
     return pl.pallas_call(
         kernel,

time: 310 us -> 232 us (0.75)
  Pallas kernels: 305 us -> 225 us
    pallas_call x1, Pallas kernels: 305 us -> 225 us  [body(): pl.pallas_call(kernel, out_shape=(jax.ShapeDtypeStruct((MATS, ROWS, R), f...]
where the time goes in v2:
time: 232 us; the launch traced here: 229 us
  Pallas kernels  225 us (97%)
  local copies, waits for them, and re-layouts  3.88 us (2%)
    pallas_call x1, Pallas kernels, body(): pl.pallas_call(kernel, out_shape=(jax.ShapeDtypeStruct((MATS, ROWS, R), f...  225 us

profile of v2, /device:TPU:1, one launch (start us, length us, event | category | flops | bytes accessed | tf_op | source)
XLA Modules:
  0.0 229.4 jit_solution(14395305177057902515)
XLA Ops:
  0.6 224.9 %sketch_project.1 = (f32[2,64,512]{2,1,0:T(8,128)}, f32[2,64,1848]{2,1,0:T(8,128)}) custom-call(bf16[2,64,29568]{2,1,0:T(8,128)(2,1)} %base_ref.1, bf16[2,64,29568]{2,1,0:T(8,128)(2,1)} %adjusted_ref.1, bf16[1848,512]{1,0:T(8,128)(2,1)} %omega_ref.1), custom_call_target="tpu_custom_call" | custom-call | flops 10000000000 | bytes 20000000 | tf_op jit(solution)/shard_map/sketch_project/pallas_call | solution.py:661
  225.5 1.7 copy.7
  227.2 2.2 copy.8

commit v3 on v2

--- a/solution.py
+++ b/solution.py
@@ -104,7 +104,7 @@
         t, g, u, near = s % 3, s // 3, (s + 4) % 16, s // 12
         dx = (1 + 2 * t - 3 * (t // 2)) * (1 - near)
         dz = ((g + 1) % 2) * (1 - near) + ((u + 1) % 2) * near
-        dk = (g // 2) * (1 - near) + (((u + 1) // 2) % 2) * near
+        dk = (1 - g // 2) * (1 - near) + (((u + 1) // 2) % 2) * near
         return dx, dz, dk
 
     def place(m, s, sign):
@@ -121,14 +121,17 @@
         return device(*place(m, s, sign))
 
     def turned(x_, y_, k_):
-        return (x_ + y_ * (1 - 2 * k_) + 4) % 4
+        return (x_ + y_ + 2 * k_) % 4
+
+    def turned_from(x_, y_, k_):
+        return (x_ - y_ - 2 * k_ + 8) % 4
 
     def block_of(m, s):
         x_, y_, z_, k_ = place(m, s, 1)
         return col_of(z_ % 2, (1 - m) * x_ + m * turned(x_, y_, k_), k_)
 
-    mine_steps = (0, 1, 2, 3, 4, 5, 12, 15)
-    twin_steps = (6, 7, 8, 9, 10, 11, 14, 13)
+    mine_steps = (6, 7, 8, 9, 10, 11, 12, 15)
+    twin_steps = (0, 1, 2, 3, 4, 5, 14, 13)
 
     def plane(q_):
         y_, z_ = q_ // 4, q_ % 4
@@ -148,7 +151,7 @@
         for copy in pending:
             copy.wait_send()
 
-        @pl.when(omega_sends > 0)
+        @pl.when(still == 0)
         def _():
             omega_copy(omega_to).wait_send()
 
@@ -191,13 +194,13 @@
 
     def holder(of):
         y_ = of // 2
-        return device((x - y_ * (1 - 2 * k) + 4) % 4, y_, (of % 2) * 2 + z_lo, k)
-
-    at_zero = 1 - (y + 3) // 4
+        return device(turned_from(x, y_, k), y_, (of % 2) * 2 + z_lo, k)
+
+    still = 1 - ((y + 2 * k) % 4 + 3) // 4
     for d in range(8):
         to = xor(r, d, 3)
         if d == 0:
-            @pl.when(y > 0)
+            @pl.when(still == 0)
             def _():
                 greet(owner(to))
                 greet(holder(to))
@@ -231,7 +234,7 @@
                     put(m, (t - 1) * TILE, value.astype(jnp.bfloat16))
                 last = tile
 
-    pl.semaphore_wait(barrier, 3 * (COLS - 1) + 16 - 2 * at_zero)
+    pl.semaphore_wait(barrier, 3 * (COLS - 1) + 16 - 2 * still)
 
     def omega_copy(to):
         return pltpu.make_async_remote_copy(
@@ -243,17 +246,14 @@
             device_id_type=MESH,
         )
 
-    from_zero = (y // 2) * (1 - y % 2) * k
-    to_two = at_zero * k
-    omega_to = device((x - y * (1 - 2 * k) + 2 * to_two + 4) % 4, y + 2 * to_two, z, k)
-    omega_sends = (1 - at_zero) * (1 - from_zero) + to_two
+    omega_to = device(turned_from(x, y, k), y, z, k)
     own_omega = pltpu.make_async_copy(omega_pad.at[0], omega_pad.at[1], own_sem)
 
-    @pl.when(omega_sends > 0)
+    @pl.when(still == 0)
     def _():
         omega_copy(omega_to).start()
 
-    @pl.when(at_zero > 0)
+    @pl.when(still > 0)
     def _():
         own_omega.start()
 
@@ -322,12 +322,8 @@
         block = held[m, first : first + count].reshape(count * ROWS, WIDE)
         return dot_nn(block, omega_pad[m]).reshape(count, ROWS, R)
 
-    def near_step(m, carry):
-        keep[m, 0:6] = sketch(m, 0, 6)
-        return carry
-
     def far_step(m, carry):
-        odd[m, 0:6] = sketch(m, 6, 6)
+        odd[m, 0:6] = sketch(m, 0, 6)
         odd_copy(m, 0).start()
         return carry
 
@@ -338,6 +334,10 @@
         odd_copy(m, 1).start()
         keep[m, 6] = got[0]
         keep[m, 7] = got[3]
+        return carry
+
+    def near_step(m, carry):
+        keep[m, 0:6] = sketch(m, 6, 6)
         odd_copy(m, 0).wait_recv()
         for e in range(6):
             keep[m, e] = keep[m, e] + pre[m, e]
@@ -351,19 +351,20 @@
         keep[m, 7] = keep[m, 7] + pre[m, 7]
         return carry
 
-    near_step(0, 0)
-
-    @pl.when(at_zero > 0)
+    @pl.when(still > 0)
     def _():
         own_omega.wait()
 
-    @pl.when(at_zero == 0)
+    @pl.when(still == 0)
     def _():
         omega_copy(omega_to).wait_recv()
 
-    near_step(1, 0)
-    for step in (far_step, last_step, close_step):
-        lax.fori_loop(0, MATS, step, 0)
+    def sketch_step(i, carry):
+        for step in (far_step, last_step, close_step, near_step):
+            step(1 - i, carry)
+        return carry
+
+    lax.fori_loop(0, MATS, sketch_step, 0)
     pending += [odd_copy(m, g) for m in range(MATS) for g in range(2)]
     pending += [part_copy(m, e) for m in range(MATS) for e in range(7)]
 
@@ -556,7 +557,7 @@
         for m in range(MATS)
     ]
 
-    for m in range(MATS):
+    for m in (1, 0):
         factor, every = inv[m], rows_all[:, m].reshape(COLS * ROWS, R)
         factor_hi, every_hi = factor.astype(jnp.bfloat16), every.astype(jnp.bfloat16)
         factor_lo = (factor - f32(factor_hi)).astype(jnp.bfloat16)
@@ -580,11 +581,11 @@
         for d in range(1, 8):
             out_copy(m, d).start()
         if m:
-            @pl.when(at_zero > 0)
+            @pl.when(still > 0)
             def _():
                 own_out[1].start()
 
-            @pl.when(at_zero == 0)
+            @pl.when(still == 0)
             def _():
                 out_copy(1, 0).start()
         else:
@@ -594,13 +595,13 @@
     for m in range(MATS):
         basis_ref[m] = dot_nt(rows_all[COLS - 1, m], inv[m], HIGH)
 
-    for m in range(MATS):
+    for m in (1, 0):
         if m:
-            @pl.when(at_zero > 0)
+            @pl.when(still > 0)
             def _():
                 own_out[1].wait()
 
-            @pl.when(at_zero == 0)
+            @pl.when(still == 0)
             def _():
                 out_arrival(1, r).wait_recv()
         else:
@@ -613,7 +614,7 @@
         projected_ref[m] = value[:, :BLOCK] * (1.0 / math.sqrt(D))
 
 
-    @pl.when(at_zero == 0)
+    @pl.when(still == 0)
     def _():
         out_copy(1, 0).wait_send()
 

time: 232 us -> 223 us (0.961); the launches traced: 229 us -> 223 us
  Pallas kernels: 225 us -> 219 us
    pallas_call x1, Pallas kernels: 225 us -> 219 us  [body(): pl.pallas_call(kernel, out_shape=(jax.ShapeDtypeStruct((MATS, ROWS, R), f...]
where the time goes in v3:
time: 223 us
  Pallas kernels  219 us (98%)
  local copies, waits for them, and re-layouts  3.88 us (2%)
    pallas_call x1, Pallas kernels, body(): pl.pallas_call(kernel, out_shape=(jax.ShapeDtypeStruct((MATS, ROWS, R), f...  219 us

profile of v3, /device:TPU:1, one launch (start us, length us, event | category | flops | bytes accessed | tf_op | source)
XLA Modules:
  0.0 223.2 jit_solution(17244354428900133086)
XLA Ops:
  0.6 218.7 %sketch_project.1 = (f32[2,64,512]{2,1,0:T(8,128)}, f32[2,64,1848]{2,1,0:T(8,128)}) custom-call(bf16[2,64,29568]{2,1,0:T(8,128)(2,1)} %base_ref.1, bf16[2,64,29568]{2,1,0:T(8,128)(2,1)} %adjusted_ref.1, bf16[1848,512]{1,0:T(8,128)(2,1)} %omega_ref.1), custom_call_target="tpu_custom_call" | custom-call | flops 10000000000 | bytes 20000000 | tf_op jit(solution)/shard_map/sketch_project/pallas_call | solution.py:662
  219.3 1.7 copy.7
  221.0 2.2 copy.8

commit v4 on v3

--- a/solution.py
+++ b/solution.py
@@ -482,54 +482,63 @@
             top = TILE * j + p * h
             gram[top : top + h, TILE * j : TILE * j + TILE] = spread[p, at : at + h, :]
 
-    low[...] = jnp.zeros((R, R), jnp.float32)
     inv[k] = jnp.zeros((R, R), jnp.float32)
-    row_at = lax.broadcasted_iota(jnp.int32, (R, TILE), 0)
+
+    def inv_copy(b):
+        span = pl.ds(b * TILE, TILE)
+        return pltpu.make_async_remote_copy(
+            src_ref=inv.at[k, span],
+            dst_ref=inv.at[k, span],
+            send_sem=inv_send.at[b],
+            recv_sem=inv_recv.at[b],
+            device_id=twin,
+            device_id_type=MESH,
+        )
+
+    def inv_arrival(b):
+        span = pl.ds(b * TILE, TILE)
+        return pltpu.make_async_remote_copy(
+            src_ref=inv.at[1 - k, span],
+            dst_ref=inv.at[1 - k, span],
+            send_sem=inv_send.at[b],
+            recv_sem=inv_recv.at[b],
+            device_id=twin,
+            device_id_type=MESH,
+        )
 
     def factor_step(b, carry):
         span = pl.ds(pl.multiple_of(b * TILE, TILE), TILE)
         own = invert_factor(gram[span, span])
-        panel = dot_nt(gram[:, span], own, HIGH)
-        panel = jnp.where(row_at >= (b + 1) * TILE, panel, 0.0)
-        done = dot_nn(low[span, :], inv[k], HIGH)
-        inv[k, span, :] = -dot_nn(own, done, HIGH)
         inv[k, span, span] = own
-        low[:, span] = panel
-        gram[...] = gram[...] - dot_nt(panel, panel, HIGH)
-
-        @pl.when(b == 2)
-        def _():
-            for e in range(7):
-                for m in range(MATS):
-                    rows_copy(m, e).wait_recv()
-                rows_core(e).start()
+        for at in range(4):
+            top, end = TILE * at, TILE * (at + 1)
+
+            @pl.when(b == at)
+            def _():
+                if at < 3:
+                    panel = dot_nt(gram[end:, top:end], own, HIGH)
+                    low[end:, top:end] = panel
+                    gram[end:, end:] = gram[end:, end:] - dot_nt(panel, panel, HIGH)
+                if at > 0:
+                    done = dot_nn(low[top:end, :top], inv[k, :top, :top], HIGH)
+                    inv[k, top:end, :top] = -dot_nn(own, done, HIGH)
+                inv_copy(at).start()
+                if at == 2:
+                    for e in range(7):
+                        for m in range(MATS):
+                            rows_copy(m, e).wait_recv()
+                        rows_core(e).start()
 
         return carry
 
     lax.fori_loop(0, R // TILE, factor_step, 0)
     pending += [rows_core(e) for e in range(7)]
-
-    inv_copy = pltpu.make_async_remote_copy(
-        src_ref=inv.at[k],
-        dst_ref=inv.at[k],
-        send_sem=inv_send,
-        recv_sem=inv_recv,
-        device_id=twin,
-        device_id_type=MESH,
-    )
-    inv_arrival = pltpu.make_async_remote_copy(
-        src_ref=inv.at[1 - k],
-        dst_ref=inv.at[1 - k],
-        send_sem=inv_send,
-        recv_sem=inv_recv,
-        device_id=twin,
-        device_id_type=MESH,
-    )
-    inv_copy.start()
-    pending.append(inv_copy)
+    pending += [inv_copy(b) for b in range(4)]
+
     for e in range(7):
         rows_core(e).wait_recv()
-    inv_arrival.wait_recv()
+    for b in range(4):
+        inv_arrival(b).wait_recv()
 
     def out_copy(m, d):
         to = xor(r, d, 3)
@@ -656,7 +665,7 @@
         sem((16,)), sem((16,)),
         sem((4,)), sem((4,)),
         sem((16,)), sem((16,)),
-        sem, sem,
+        sem((4,)), sem((4,)),
         sem((MATS, 8)), sem((MATS, 8)), sem((MATS,)),
     ]
     return pl.pallas_call(

time: 223 us -> 217 us (0.973)
  Pallas kernels: 219 us -> 213 us
    pallas_call x1, Pallas kernels: 219 us -> 213 us  [body(): pl.pallas_call(kernel, out_shape=(jax.ShapeDtypeStruct((MATS, ROWS, R), f...]
where the time goes in v4:
time: 217 us
  Pallas kernels  213 us (98%)
  local copies, waits for them, and re-layouts  3.88 us (2%)
    pallas_call x1, Pallas kernels, body(): pl.pallas_call(kernel, out_shape=(jax.ShapeDtypeStruct((MATS, ROWS, R), f...  213 us

profile of v4, /device:TPU:1, one launch (start us, length us, event | category | flops | bytes accessed | tf_op | source)
XLA Modules:
  0.0 217.0 jit_solution(3026517370403682568)
XLA Ops:
  0.6 212.5 %sketch_project.1 = (f32[2,64,512]{2,1,0:T(8,128)}, f32[2,64,1848]{2,1,0:T(8,128)}) custom-call(bf16[2,64,29568]{2,1,0:T(8,128)(2,1)} %base_ref.1, bf16[2,64,29568]{2,1,0:T(8,128)(2,1)} %adjusted_ref.1, bf16[1848,512]{1,0:T(8,128)(2,1)} %omega_ref.1), custom_call_target="tpu_custom_call" | custom-call | flops 10000000000 | bytes 20000000 | tf_op jit(solution)/shard_map/sketch_project/pallas_call | solution.py:671
  213.1 1.7 copy.7
  214.8 2.2 %copy.8 = f32[2,64,1848]{2,1,0:T(8,128)} copy(f32[2,64,1848]{2,1,0:T(8,128)} %get-tuple-element.5) | data formatting | bytes 1892352

commit v5 on v4

--- a/solution.py
+++ b/solution.py
@@ -540,23 +540,25 @@
     for b in range(4):
         inv_arrival(b).wait_recv()
 
-    def out_copy(m, d):
+    halves = (pl.ds(0, 1152), pl.ds(1152, 768))
+
+    def out_copy(m, d, h):
         to = xor(r, d, 3)
         return pltpu.make_async_remote_copy(
-            src_ref=out_part.at[m, to],
-            dst_ref=in_part.at[m, r],
-            send_sem=out_send.at[m, d],
-            recv_sem=out_recv.at[m, r],
+            src_ref=out_part.at[m, to, :, halves[h]],
+            dst_ref=in_part.at[m, r, :, halves[h]],
+            send_sem=out_send.at[m, d, h],
+            recv_sem=out_recv.at[m, r, h],
             device_id=owner(to) if m else (to, c),
             device_id_type=MESH,
         )
 
-    def out_arrival(m, d):
-        return pltpu.make_async_remote_copy(
-            src_ref=out_part.at[m, d],
-            dst_ref=in_part.at[m, d],
-            send_sem=out_send.at[m, 0],
-            recv_sem=out_recv.at[m, d],
+    def out_arrival(m, d, h):
+        return pltpu.make_async_remote_copy(
+            src_ref=out_part.at[m, d, :, halves[h]],
+            dst_ref=in_part.at[m, d, :, halves[h]],
+            send_sem=out_send.at[m, 0, h],
+            recv_sem=out_recv.at[m, d, h],
             device_id=holder(d) if m else (d, c),
             device_id_type=MESH,
         )
@@ -586,20 +588,21 @@
             out_part[m, :, :, span] = got.reshape(8, ROWS, 384).astype(jnp.bfloat16)
             return carry
 
-        lax.fori_loop(0, WIDE // 384, project_step, 0)
-        for d in range(1, 8):
-            out_copy(m, d).start()
+        for h, (begin, end) in enumerate(((0, 3), (3, 5))):
+            lax.fori_loop(begin, end, project_step, 0)
+            for d in range(1, 8):
+                out_copy(m, d, h).start()
+            if m:
+                @pl.when(still == 0)
+                def _():
+                    out_copy(1, 0, h).start()
         if m:
             @pl.when(still > 0)
             def _():
                 own_out[1].start()
-
-            @pl.when(still == 0)
-            def _():
-                out_copy(1, 0).start()
         else:
             own_out[0].start()
-    pending += [out_copy(m, d) for m in range(MATS) for d in range(1, 8)]
+    pending += [out_copy(m, d, h) for m in range(MATS) for d in range(1, 8) for h in range(2)]
 
     for m in range(MATS):
         basis_ref[m] = dot_nt(rows_all[COLS - 1, m], inv[m], HIGH)
@@ -612,11 +615,13 @@
 
             @pl.when(still == 0)
             def _():
-                out_arrival(1, r).wait_recv()
+                for h in range(2):
+                    out_arrival(1, r, h).wait_recv()
         else:
             own_out[0].wait()
         for d in range(1, 8):
-            out_arrival(m, xor(r, d, 3)).wait_recv()
+            for h in range(2):
+                out_arrival(m, xor(r, d, 3), h).wait_recv()
         value = f32(in_part[m, 0])
         for d in range(1, 8):
             value = value + f32(in_part[m, d])
@@ -625,7 +630,8 @@
 
     @pl.when(still == 0)
     def _():
-        out_copy(1, 0).wait_send()
+        for h in range(2):
+            out_copy(1, 0, h).wait_send()
 
     finish()
 
@@ -666,7 +672,7 @@
         sem((4,)), sem((4,)),
         sem((16,)), sem((16,)),
         sem((4,)), sem((4,)),
-        sem((MATS, 8)), sem((MATS, 8)), sem((MATS,)),
+        sem((MATS, 8, 2)), sem((MATS, 8, 2)), sem((MATS,)),
     ]
     return pl.pallas_call(
         kernel,

time: 217 us -> 208 us (0.959)
  Pallas kernels: 213 us -> 203 us
    pallas_call x1, Pallas kernels: 213 us -> 203 us  [body(): pl.pallas_call(kernel, out_shape=(jax.ShapeDtypeStruct((MATS, ROWS, R), f...]
where the time goes in v5:
time: 208 us; the launch traced here: 207 us
  Pallas kernels  203 us (98%)
  local copies, waits for them, and re-layouts  3.88 us (2%)
    pallas_call x1, Pallas kernels, body(): pl.pallas_call(kernel, out_shape=(jax.ShapeDtypeStruct((MATS, ROWS, R), f...  203 us

profile of v5, /device:TPU:1, one launch (start us, length us, event | category | flops | bytes accessed | tf_op | source)
XLA Modules:
  0.0 207.2 jit_solution(2567292504262633968)
XLA Ops:
  0.6 202.7 %sketch_project.1 = (f32[2,64,512]{2,1,0:T(8,128)}, f32[2,64,1848]{2,1,0:T(8,128)}) custom-call(bf16[2,64,29568]{2,1,0:T(8,128)(2,1)} %base_ref.1, bf16[2,64,29568]{2,1,0:T(8,128)(2,1)} %adjusted_ref.1, bf16[1848,512]{1,0:T(8,128)(2,1)} %omega_ref.1), custom_call_target="tpu_custom_call" | custom-call | flops 10000000000 | bytes 20000000 | tf_op jit(solution)/shard_map/sketch_project/pallas_call | solution.py:677
  203.3 1.7 copy.7
  205.0 2.2 %copy.8 = f32[2,64,1848]{2,1,0:T(8,128)} copy(f32[2,64,1848]{2,1,0:T(8,128)} %get-tuple-element.5) | data formatting | bytes 1892352
